TPU v7x, 256 devices: a whole 4x4x8 slice. The times are simulated.
256 devices in a mesh: out: 16 (over y, x), inp: 16 (over z, core).
Axes of the slice: x: 4, y: 4, z: 8, core: 2. Of those that a mesh axis runs over, the one named last changes fastest.
Arguments:
- grads: bfloat16 [2048, 28672], P('out', 'inp'), may hold values from -1.1953125 to 1.1953125
- acts: bfloat16 [2048, 8192], P('inp', 'out'), may hold values from -6 to 6
- basis_out: bfloat16 [28672, 14336], P('inp', 'out'), may hold values from -0.03125 to 0.03125
- basis_in: bfloat16 [8192, 8192], P('out', 'inp'), may hold values from -0.0625 to 0.0625
- old_correction: float32 [14336, 8192], P('out', 'inp'), may hold values from 0.1 to 2
- lengths: int32 [16], replicated, may hold values from 1 to 256, 2048 in all
Outputs:
- correction: float32 [14336, 8192], P('out', 'inp')
Inputs may be any that keep to these rules, and one draw needn't show every extreme that they name: The lengths sum to 2048; the longest example has exactly 256 tokens.
All inputs are finite; a program needn't handle non-finite values.
Results may differ from a plain program's by a relative error of at most 0.0021.
Values may be sent and summed in bfloat16 or wider, within the bound.
No kernel may reach another device: no remote copies, remote signals or barrier semaphores. Data moves between devices by JAX's collectives and lax.ppermute only.
A program may use at most 128 MiB of HBM per device.

v0:
```python
import jax
import jax.numpy as jnp
from jax import lax
from jax.sharding import PartitionSpec as P

CAP = 256


def body(grads, acts, basis_out, basis_in, old_correction, lengths):
    gathered = lax.all_gather(grads, "out", axis=0, tiled=True)
    row_count = gathered.shape[0]
    scattered = lax.psum_scatter(
        lax.dot_general(
            basis_out, gathered, (((0,), (1,)), ((), ())), preferred_element_type=jnp.float32
        ),
        "inp",
        scatter_dimension=0,
        tiled=True,
    )
    grad_rot = lax.all_gather(scattered.astype(jnp.bfloat16), "inp", axis=0, tiled=True)
    token_dim = 1
    gathered_acts = lax.all_gather(acts, "inp", axis=0, tiled=True)
    act_scattered = lax.psum_scatter(
        jnp.dot(gathered_acts, basis_in, preferred_element_type=jnp.float32),
        "out",
        scatter_dimension=0,
        tiled=True,
    )
    act_rot = lax.all_gather(act_scattered.astype(jnp.bfloat16), "out", axis=0, tiled=True)
    offsets = jnp.cumsum(lengths) - lengths
    examples = lengths.shape[0]

    def add_example(example, running):
        offset = offsets[example]
        length = lengths[example]
        first_row = jnp.minimum(offset, row_count - CAP)
        places = first_row + jnp.arange(CAP, dtype=jnp.int32)
        inside = (places >= offset) & (places < offset + length)
        grad_block = lax.dynamic_slice_in_dim(grad_rot, first_row, CAP, token_dim)
        act_block = lax.dynamic_slice_in_dim(act_rot, first_row, CAP, 0)
        act_block = jnp.where(inside[:, None], act_block, jnp.zeros((), act_block.dtype))
        projected = lax.dot_general(
            grad_block,
            act_block,
            (((token_dim,), (0,)), ((), ())),
            preferred_element_type=jnp.float32,
        )
        return running + projected * projected

    running = lax.fori_loop(0, examples, add_example, jnp.zeros(old_correction.shape, jnp.float32))
    return 0.8 * old_correction + 0.2 * running / examples


def solution(mesh):
    in_specs = (
        P("out", "inp"),
        P("inp", "out"),
        P("inp", "out"),
        P("out", "inp"),
        P("out", "inp"),
        P(),
    )
    out_specs = P("out", "inp")
    return jax.shard_map(body, mesh=mesh, in_specs=in_specs, out_specs=out_specs, check_vma=False)
```

profile of v0, /device:TPU:1, one launch (start us, length us, event | category | flops | bytes accessed | tf_op | source)
XLA Modules:
  0.0 505.1 jit_solution(16237639878966446037)
XLA Ops:
  6.5 0.7 all-gather.9.cloned.1.call-update
  7.3 0.7 all-gather.5.cloned.1.call-update
  8.1 45.1 %all-gather.9.cloned.1.call-done = bf16[2048,512]{1,0:T(8,128)(2,1)} async-done(((bf16[128,512]{1,0:T(8,128)(2,1)}), bf16[2048,512]{1,0:T(8,128)(2,1)}) %all-gather.9.cloned.1.call-update) | async-done | bytes 2097168 | tf_op jit(solution)/shard_map/all_gather | solution.py:22
  53.2 4.9 fusion.8
  58.1 66.5 %all-gather.5.cloned.1.call-done = bf16[2048,1792]{1,0:T(8,128)(2,1)} async-done(((bf16[128,1792]{1,0:T(8,128)(2,1)}), bf16[2048,1792]{1,0:T(8,128)(2,1)}) %all-gather.5.cloned.1.call-update) | async-done | bytes 7340048 | tf_op jit(solution)/shard_map/all_gather | solution.py:10
  124.7 10.9 %fusion.7 = f32[896,2048]{1,0:T(8,128)} fusion(bf16[1792,896]{1,0:T(8,128)(2,1)S(1)} %copy-done, bf16[2048,1792]{1,0:T(8,128)(2,1)} %all-gather.5.cloned.1.call-done), kind=kOutput, calls=%fused_computation.10 | convolution fusion | flops 6576668672 | bytes 17891328 | tf_op jit(solution)/shard_map/dot_general | solution.py:13
  135.7 73.4 %reduce-scatter.5.cloned.1.call-done = f32[128,512]{1,0:T(8,128)} async-done(((f32[2048,512]{1,0:T(8,128)}), f32[128,512]{1,0:T(8,128)}) %reduce-scatter.5.cloned.1.call-update) | async-done | bytes 262160 | tf_op jit(solution)/shard_map/reduce_scatter | solution.py:23
  209.1 1.6 convert_element_type.7
  210.8 67.7 %reduce-scatter.3.cloned.1.call-done = f32[56,2048]{1,0:T(8,128)} async-done(((f32[896,2048]{1,0:T(8,128)}), f32[56,2048]{1,0:T(8,128)}) %reduce-scatter.3.cloned.1.call-update) | async-done | bytes 458768 | tf_op jit(solution)/shard_map/reduce_scatter | solution.py:12
  278.4 1.7 convert_element_type.6
  280.5 51.2 %all-gather.11.cloned.1.call-done = bf16[2048,512]{1,0:T(8,128)(2,1)} async-done(((bf16[128,512]{1,0:T(8,128)(2,1)}), bf16[2048,512]{1,0:T(8,128)(2,1)}) %all-gather.11.cloned.1.call-update) | async-done | bytes 2097168 | tf_op jit(solution)/shard_map/all_gather | solution.py:29
  331.6 44.1 %all-gather.7.cloned.1.call-done = bf16[896,2048]{1,0:T(8,128)(2,1)} async-done(((bf16[56,2048]{1,0:T(8,128)(2,1)}), bf16[896,2048]{1,0:T(8,128)(2,1)}) %all-gather.7.cloned.1.call-update) | async-done | bytes 3670032 | tf_op jit(solution)/shard_map/all_gather | solution.py:20
  375.7 118.8 %while.14 = (s32[]{:T(128)}, f32[896,512]{1,0:T(8,128)}, s32[16]{0:T(128)S(1)}, bf16[896,2048]{1,0:T(8,128)(2,1)}, s32[16]{0:T(128)S(1)}, /*index=5*/bf16[2048,5...) while((s32[]{:T(128)}, f32[896,512]{1,0:T(8,128)}, s32[16]{0:T(128)S(1)}, ...), condition=%wide.region_4.5_spmd.clone, body=%wide.region_3.4_spmd.clone.sunk | while | flops 236389376 | bytes 4393164 | solution.py:50
  379.7 2.9 select_add_fusion.2
  385.8 0.7 compare_and_fusion.2
  386.5 3.5 select_add_fusion.2
  393.3 0.7 compare_and_fusion.2
  394.0 3.5 select_add_fusion.2
  401.5 3.5 select_add_fusion.2
  408.9 3.5 select_add_fusion.2
  416.4 3.5 select_add_fusion.2
  423.9 3.5 select_add_fusion.2
  431.4 3.5 select_add_fusion.2
  438.9 3.5 select_add_fusion.2
  446.3 3.5 select_add_fusion.2
  453.8 3.5 select_add_fusion.2
  461.3 3.5 select_add_fusion.2
  468.8 3.5 select_add_fusion.2
  476.3 3.5 select_add_fusion.2
  483.7 3.5 select_add_fusion.2
  491.1 3.5 select_add_fusion.2
  494.6 3.7 multiply_add_fusion
  (65 shorter events, 30.4 us)
Async XLA Ops:
  6.5 118.1 %copy-start = (bf16[1792,896]{1,0:T(8,128)(2,1)S(1)}, bf16[1792,896]{1,0:T(8,128)(2,1)}, u32[]{:S(2)}) copy-start(bf16[1792,896]{1,0:T(8,128)(2,1)} %param.10) | copy-start | bytes 9633796
  6.5 46.6 %all-gather.9.cloned.1.call-start = ((), (), s32[]{:S(2)}) async-start(), calls=%async_computation.5 | async-start | bytes 2228224 | tf_op jit(solution)/shard_map/all_gather | solution.py:22
  7.3 117.4 %all-gather.5.cloned.1.call-start = ((), (), s32[]{:S(2)}) async-start(), calls=%async_computation.2 | async-start | bytes 7798784 | tf_op jit(solution)/shard_map/all_gather | solution.py:10
  8.0 201.1 %reduce-scatter.5.cloned.1.call-start = ((), (), s32[]{:S(2)}) async-start(), calls=%async_computation.6 | async-start | bytes 4456448 | tf_op jit(solution)/shard_map/reduce_scatter | solution.py:23
  58.1 220.3 %reduce-scatter.3.cloned.1.call-start = ((), (), s32[]{:S(2)}) async-start(), calls=%async_computation.3 | async-start | bytes 7798784 | tf_op jit(solution)/shard_map/reduce_scatter | solution.py:12
  135.6 144.6 %copy-start.1 = (s32[16]{0:T(128)S(1)}, s32[16]{0:T(128)}, u32[]{:S(2)}) copy-start(s32[16]{0:T(128)} %param.13) | copy-start | bytes 196
  135.6 196.0 %all-gather.11.cloned.1.call-start = ((), (), s32[]{:S(2)}) async-start(), calls=%async_computation.7 | async-start | bytes 2228224 | tf_op jit(solution)/shard_map/all_gather | solution.py:29
  210.7 165.0 %all-gather.7.cloned.1.call-start = ((), (), s32[]{:S(2)}) async-start(), calls=%async_computation.4 | async-start | bytes 3899392 | tf_op jit(solution)/shard_map/all_gather | solution.py:20
Sparse Core Ops, SparseCore 0:
  9.2 43.9 all-gather.8
  55.6 69.0 all-gather.4
  128.3 80.7 reduce-scatter.4
  211.7 66.7 reduce-scatter.2
  281.0 50.5 all-gather.10
  333.5 42.2 all-gather.6
where the time goes:
time: 506 us; the launch traced here: 505 us
  waiting for transfers between devices  349 us (69%)
  matrix products  71.7 us (14%)
  loops' own time  31.7 us (6%)
  local copies, waits for them, and re-layouts  20.2 us (4%)
  other arithmetic  18.3 us (4%)
  between operations  13.5 us (3%)
    reduce_scatter x1, waiting for transfers between devices, body(): lax.psum_scatter(jnp.dot(gathered_acts, basis_in, preferred_element_type=...  73.4 us
    reduce_scatter x1, waiting for transfers between devices, body(): lax.psum_scatter(lax.dot_general(basis_out, gathered, (((0,), (1,)), ((),...  67.7 us
    all_gather x1, waiting for transfers between devices, body(): gathered = lax.all_gather(grads, 'out', axis=0, tiled=True)  66.5 us
    dot_general x16, matrix products, add_example(): lax.dot_general(grad_block, act_block, (((token_dim,), (0,)), ((), ())),...  55.9 us
    all_gather x1, waiting for transfers between devices, body(): lax.all_gather(act_scattered.astype(jnp.bfloat16), 'out', axis=0, tiled=T...  51.2 us
    all_gather x1, waiting for transfers between devices, body(): gathered_acts = lax.all_gather(acts, 'inp', axis=0, tiled=True)  45.1 us
    all_gather x1, waiting for transfers between devices, body(): lax.all_gather(scattered.astype(jnp.bfloat16), 'inp', axis=0, tiled=True)  44.1 us
    another operation x1, loops' own time, body(): lax.fori_loop(0, examples, add_example, jnp.zeros(old_correction.shape, j...  31.7 us
  transfers between devices with their start and end apart: 6, of which 6 were waited for; matrix products, arithmetic and copies ran while one was open for 4% of the time, Pallas kernels for 0%

commit v1 on v0

--- a/solution.py
+++ b/solution.py
@@ -6,8 +6,37 @@
 CAP = 256
 
 
+def report_the_tracks(u_in, dim_no):
+    u_in = jnp.moveaxis(u_in, 0, dim_no)
+    k_now = u_in.shape
+    return u_in.reshape(*k_now[:dim_no], k_now[dim_no] * k_now[dim_no + 1], *k_now[dim_no + 2 :])
+
+
 def body(grads, acts, basis_out, basis_in, old_correction, lengths):
-    gathered = lax.all_gather(grads, "out", axis=0, tiled=True)
+
+    def masks_direct(array_here, comm_axis, axis_no):
+        n_shards = lax.axis_size(comm_axis)
+        seen = [(i, (i + 1) % n_shards) for i in range(n_shards)]
+        xs_all = [(w, dd) for dd, w in seen]
+        current_value, answer = ([], [])
+        p = 0
+        while p < n_shards - 1:
+            if p % 2 == 0:
+                current_value.append(
+                    lax.ppermute(
+                        current_value[-1] if current_value else array_here, comm_axis, seen
+                    )
+                )
+            else:
+                answer.append(lax.ppermute(answer[-1] if answer else array_here, comm_axis, xs_all))
+            p += 1
+        last = jnp.stack([*current_value[::-1], array_here, *answer])
+        everything = lax.axis_index(comm_axis)
+        main = everything - len(current_value)
+        last = last[(jnp.arange(n_shards) - main) % n_shards]
+        return report_the_tracks(last, axis_no)
+
+    gathered = masks_direct(grads, "out", 0)
     row_count = gathered.shape[0]
     scattered = lax.psum_scatter(
         lax.dot_general(

time: 506 us -> 498 us (0.984)
  waiting for transfers between devices: 349 us -> 259 us
  local copies, waits for them, and re-layouts: 20.2 us -> 65.1 us
  starting transfers between devices: 0.2 us -> 37.6 us
    all_gather x1 -> x0, waiting for transfers between devices: 66.5 us -> none  [body(): gathered = lax.all_gather(grads, 'out', axis=0, tiled=True)]
    ppermute x0 -> x15, waiting for transfers between devices: none -> 57.6 us  [the longest x8 53.8 us: masks_direct(): lax.ppermute(current_value[-1] if current_value else array_here, comm_axi...]
    all_gather x1, waiting for transfers between devices: 45.1 us -> 0.01 us  [body(): gathered_acts = lax.all_gather(acts, 'inp', axis=0, tiled=True)]
    ppermute x0 -> x15, starting transfers between devices: none -> 37.4 us  [the longest x7 35.4 us: masks_direct(): lax.ppermute(answer[-1] if answer else array_here, comm_axis, xs_all)]
    unnamed x4 -> x42, local copies, waits for them, and re-layouts: 0.01 us -> 35.6 us
    reduce_scatter x1, waiting for transfers between devices: 73.4 us -> 38.6 us  [body(): lax.psum_scatter(jnp.dot(gathered_acts, basis_in, preferred_element_type=...]
    gather x0 -> x1, local copies, waits for them, and re-layouts: none -> 7.15 us  [masks_direct(): last = last[(jnp.arange(n_shards) - main) % n_shards]]
  transfers between devices with their start and end apart: 6 -> 20, of which waited for: 6 -> 16; matrix products, arithmetic and copies ran while one was open for 4% -> 13% of each run, Pallas kernels for 0% -> 0%
where the time goes in v1:
time: 498 us; the launch traced here: 496 us
  waiting for transfers between devices  259 us (52%)
  matrix products  72.8 us (15%)
  local copies, waits for them, and re-layouts  65.1 us (13%)
  starting transfers between devices  37.6 us (8%)
  loops' own time  30.9 us (6%)
  other arithmetic  17 us (3%)
  between operations  13.2 us (3%)
    reduce_scatter x1, waiting for transfers between devices, body(): lax.psum_scatter(lax.dot_general(basis_out, gathered, (((0,), (1,)), ((),...  67.8 us
    dot_general x16, matrix products, add_example(): lax.dot_general(grad_block, act_block, (((token_dim,), (0,)), ((), ())),...  55.9 us
    ppermute x8, waiting for transfers between devices, masks_direct(): lax.ppermute(current_value[-1] if current_value else array_here, comm_axi...  53.8 us
    all_gather x1, waiting for transfers between devices, body(): lax.all_gather(act_scattered.astype(jnp.bfloat16), 'out', axis=0, tiled=T...  51.2 us
    all_gather x1, waiting for transfers between devices, body(): lax.all_gather(scattered.astype(jnp.bfloat16), 'inp', axis=0, tiled=True)  44.1 us
    reduce_scatter x1, waiting for transfers between devices, body(): lax.psum_scatter(jnp.dot(gathered_acts, basis_in, preferred_element_type=...  38.6 us
    unnamed x42, local copies, waits for them, and re-layouts  35.6 us
    ppermute x7, starting transfers between devices, masks_direct(): lax.ppermute(answer[-1] if answer else array_here, comm_axis, xs_all)  35.4 us
  transfers between devices with their start and end apart: 20, of which 16 were waited for; matrix products, arithmetic and copies ran while one was open for 13% of the time, Pallas kernels for 0%

profile of v1, /device:TPU:1, one launch (start us, length us, event | category | flops | bytes accessed | tf_op | source)
XLA Modules:
  0.0 496.1 jit_solution(2947978650718330207)
XLA Ops:
  8.6 12.3 %collective-permute-done = bf16[128,1792]{1,0:T(8,128)(2,1)} collective-permute-done((bf16[128,1792]{1,0:T(8,128)(2,1)}, bf16[128,1792]{1,0:T(8,128)(2,1)}, u32[]{:S(2)}, u32[]{:S(2)}) %collective-permute-start) | collective-permute-done | bytes 458784 | tf_op jit(solution)/shard_map/ppermute | solution.py:26
  21.0 4.9 collective-permute-start.8
  25.8 7.5 %collective-permute-done.1 = bf16[128,1792]{1,0:T(8,128)(2,1)} collective-permute-done((bf16[128,1792]{1,0:T(8,128)(2,1)}, bf16[128,1792]{1,0:T(8,128)(2,1)}, u32[]{:S(2)}, u32[]{:S(2)}) %collective-permute-start.1) | collective-permute-done | bytes 458784 | tf_op jit(solution)/shard_map/ppermute | solution.py:26
  34.2 4.8 collective-permute-start.9
  38.9 5.9 %collective-permute-done.2 = bf16[128,1792]{1,0:T(8,128)(2,1)S(1)} collective-permute-done((bf16[128,1792]{1,0:T(8,128)(2,1)}, bf16[128,1792]{1,0:T(8,128)(2,1)S(1)}, u32[]{:S(2)}, u32[]{:S(2)}) %collective-permute-start.2) | collective-permute-done | bytes 458784 | tf_op jit(solution)/shard_map/ppermute | solution.py:26
  45.6 4.7 collective-permute-start.10
  50.4 5.1 %collective-permute-done.3 = bf16[128,1792]{1,0:T(8,128)(2,1)S(1)} collective-permute-done((bf16[128,1792]{1,0:T(8,128)(2,1)S(1)}, bf16[128,1792]{1,0:T(8,128)(2,1)S(1)}, u32[]{:S(2)}, u32[]{:S(2)}) %collective-permute-start.3) | collective-permute-done | bytes 458784 | tf_op jit(solution)/shard_map/ppermute | solution.py:26
  55.8 5.2 %collective-permute-start.11 = (bf16[128,1792]{1,0:T(8,128)(2,1)S(1)}, bf16[128,1792]{1,0:T(8,128)(2,1)S(1)}, u32[]{:S(2)}, u32[]{:S(2)}) collective-permute-start(bf16[128,1792]{1,0:T(8,128)(2,1)S(1)} %collective-permute-done.10), channel_id=1, source_target_pairs={{16,0},{32,16},{48,32},{64,48},{80,64},{96,80},{112,96},{128,112},... | collective-permute-start | bytes 1376264 | tf_op jit(solution)/shard_map/ppermute | solution.py:31
  61.0 5.1 %collective-permute-done.4 = bf16[128,1792]{1,0:T(8,128)(2,1)S(1)} collective-permute-done((bf16[128,1792]{1,0:T(8,128)(2,1)S(1)}, bf16[128,1792]{1,0:T(8,128)(2,1)S(1)}, u32[]{:S(2)}, u32[]{:S(2)}) %collective-permute-start.4) | collective-permute-done | bytes 458784 | tf_op jit(solution)/shard_map/ppermute | solution.py:26
  67.5 5.2 %collective-permute-start.12 = (bf16[128,1792]{1,0:T(8,128)(2,1)S(1)}, bf16[128,1792]{1,0:T(8,128)(2,1)}, u32[]{:S(2)}, u32[]{:S(2)}) collective-permute-start(bf16[128,1792]{1,0:T(8,128)(2,1)S(1)} %collective-permute-done.11), channel_id=1, source_target_pairs={{16,0},{32,16},{48,32},{64,48},{80,64},{96,80},{112,96},{128,112},... | collective-permute-start | bytes 1376264 | tf_op jit(solution)/shard_map/ppermute | solution.py:31
  72.8 4.9 collective-permute-done.5
  78.8 5.3 %collective-permute-start.13 = (bf16[128,1792]{1,0:T(8,128)(2,1)}, bf16[128,1792]{1,0:T(8,128)(2,1)}, u32[]{:S(2)}, u32[]{:S(2)}) collective-permute-start(bf16[128,1792]{1,0:T(8,128)(2,1)} %collective-permute-done.12), channel_id=1, source_target_pairs={{16,0},{32,16},{48,32},{64,48},{80,64},{96,80},{112,96},{128,112},... | collective-permute-start | bytes 1376264 | tf_op jit(solution)/shard_map/ppermute | solution.py:31
  84.2 6.2 %collective-permute-done.6 = bf16[128,1792]{1,0:T(8,128)(2,1)} collective-permute-done((bf16[128,1792]{1,0:T(8,128)(2,1)S(1)}, bf16[128,1792]{1,0:T(8,128)(2,1)}, u32[]{:S(2)}, u32[]{:S(2)}) %collective-permute-start.6) | collective-permute-done | bytes 458784 | tf_op jit(solution)/shard_map/ppermute | solution.py:26
  92.1 5.2 %collective-permute-start.14 = (bf16[128,1792]{1,0:T(8,128)(2,1)}, bf16[128,1792]{1,0:T(8,128)(2,1)}, u32[]{:S(2)}, u32[]{:S(2)}) collective-permute-start(bf16[128,1792]{1,0:T(8,128)(2,1)} %collective-permute-done.13), channel_id=1, source_target_pairs={{16,0},{32,16},{48,32},{64,48},{80,64},{96,80},{112,96},{128,112},... | collective-permute-start | bytes 1376264 | tf_op jit(solution)/shard_map/ppermute | solution.py:31
  97.3 6.8 %collective-permute-done.7 = bf16[128,1792]{1,0:T(8,128)(2,1)} collective-permute-done((bf16[128,1792]{1,0:T(8,128)(2,1)}, bf16[128,1792]{1,0:T(8,128)(2,1)}, u32[]{:S(2)}, u32[]{:S(2)}) %collective-permute-start.7) | collective-permute-done | bytes 458784 | tf_op jit(solution)/shard_map/ppermute | solution.py:26
  107.8 4.9 fusion.9
  135.4 7.1 %gather_fusion = bf16[16,128,1792]{2,1,0:T(8,128)(2,1)} fusion(bf16[16,128,1792]{2,1,0:T(8,128)(2,1)} %bitcast_dynamic-update-slice_fusion, s32[1024]{0:T(1024)S(1)} %pad_clamp_fusion), kind=kCustom, calls=%fused_computation | custom fusion | bytes 14680128 | tf_op jit(solution)/shard_map/gather | solution.py:36
  142.6 12.0 %convolution_bitcast_fusion = f32[896,2048]{0,1:T(8,128)} fusion(bf16[2048,1792]{1,0:T(8,128)(2,1)} %bitcast.49, bf16[1792,896]{1,0:T(8,128)(2,1)S(1)} %copy-done), kind=kOutput, calls=%fused_computation.10 | convolution fusion | flops 6576668672 | bytes 17891328 | tf_op jit(solution)/shard_map/dot_general | solution.py:42
  154.5 8.7 %copy.15 = f32[896,2048]{1,0:T(8,128)} copy(f32[896,2048]{0,1:T(8,128)} %convolution_bitcast_fusion) | data formatting | bytes 14680064
  163.3 38.6 %reduce-scatter.5.cloned.1.call-done = f32[128,512]{1,0:T(8,128)} async-done(((f32[2048,512]{1,0:T(8,128)}), f32[128,512]{1,0:T(8,128)}) %reduce-scatter.5.cloned.1.call-update) | async-done | bytes 262160 | tf_op jit(solution)/shard_map/reduce_scatter | solution.py:52
  203.6 67.8 %reduce-scatter.7.cloned.1.call-done = f32[56,2048]{1,0:T(8,128)} async-done(((f32[896,2048]{1,0:T(8,128)}), f32[56,2048]{1,0:T(8,128)}) %reduce-scatter.7.cloned.1.call-update) | async-done | bytes 458768 | tf_op jit(solution)/shard_map/reduce_scatter | solution.py:41
  273.4 51.2 %all-gather.8.cloned.1.call-done = bf16[2048,512]{1,0:T(8,128)(2,1)} async-done(((bf16[128,512]{1,0:T(8,128)(2,1)}), bf16[2048,512]{1,0:T(8,128)(2,1)}) %all-gather.8.cloned.1.call-update) | async-done | bytes 2097168 | tf_op jit(solution)/shard_map/all_gather | solution.py:58
  324.6 44.1 %all-gather.4.cloned.1.call-done = bf16[896,2048]{1,0:T(8,128)(2,1)} async-done(((bf16[56,2048]{1,0:T(8,128)(2,1)}), bf16[896,2048]{1,0:T(8,128)(2,1)}) %all-gather.4.cloned.1.call-update) | async-done | bytes 3670032 | tf_op jit(solution)/shard_map/all_gather | solution.py:49
  368.7 117.1 %while.14 = (s32[]{:T(128)}, f32[896,512]{1,0:T(8,128)}, s32[16]{0:T(128)S(1)}, bf16[896,2048]{1,0:T(8,128)(2,1)}, s32[16]{0:T(128)S(1)}, /*index=5*/bf16[2048,5...) while((s32[]{:T(128)}, f32[896,512]{1,0:T(8,128)}, s32[16]{0:T(128)S(1)}, ...), condition=%wide.region_4.5_spmd.clone, body=%wide.region_3.4_spmd.clone.sunk | while | flops 236389376 | bytes 4393164 | solution.py:79
  394.0 3.5 select_add_fusion.2
  401.4 3.5 select_add_fusion.2
  408.8 3.5 select_add_fusion.2
  423.5 3.5 select_add_fusion.2
  438.2 3.5 select_add_fusion.2
  445.6 3.5 select_add_fusion.2
  453.0 3.5 select_add_fusion.2
  485.8 3.7 multiply_add_fusion
  (134 shorter events, 99.8 us)
Async XLA Ops:
  6.5 136.1 %copy-start = (bf16[1792,896]{1,0:T(8,128)(2,1)S(1)}, bf16[1792,896]{1,0:T(8,128)(2,1)}, u32[]{:S(2)}) copy-start(bf16[1792,896]{1,0:T(8,128)(2,1)} %param.10) | copy-start | bytes 9633796
  6.5 101.2 %all-gather.6.cloned.1.call-start = ((), (), s32[]{:S(2)}) async-start(), calls=%async_computation.3 | async-start | bytes 2228224 | tf_op jit(solution)/shard_map/all_gather | solution.py:51
  6.5 14.4 %collective-permute-start = (bf16[128,1792]{1,0:T(8,128)(2,1)}, bf16[128,1792]{1,0:T(8,128)(2,1)}, u32[]{:S(2)}, u32[]{:S(2)}) collective-permute-start(bf16[128,1792]{1,0:T(8,128)(2,1)} %param.8), channel_id=1, source_target_pairs={{0,16},{16,32},{32,48},{48,64},{64,80},{80,96},{96,112},{112,128},... | collective-permute-start | bytes 1376264 | tf_op jit(solution)/shard_map/ppermute | solution.py:26
  20.9 12.5 %collective-permute-start.1 = (bf16[128,1792]{1,0:T(8,128)(2,1)}, bf16[128,1792]{1,0:T(8,128)(2,1)}, u32[]{:S(2)}, u32[]{:S(2)}) collective-permute-start(bf16[128,1792]{1,0:T(8,128)(2,1)} %collective-permute-done), channel_id=1, source_target_pairs={{0,16},{16,32},{32,48},{48,64},{64,80},{80,96},{96,112},{112,128},... | collective-permute-start | bytes 1376264 | tf_op jit(solution)/shard_map/ppermute | solution.py:26
  20.9 181.0 %reduce-scatter.5.cloned.1.call-start = ((), (), s32[]{:S(2)}) async-start(), calls=%async_computation.4 | async-start | bytes 4456448 | tf_op jit(solution)/shard_map/reduce_scatter | solution.py:52
  21.0 12.4 %collective-permute-start.8 = (bf16[128,1792]{1,0:T(8,128)(2,1)}, bf16[128,1792]{1,0:T(8,128)(2,1)S(1)}, u32[]{:S(2)}, u32[]{:S(2)}) collective-permute-start(bf16[128,1792]{1,0:T(8,128)(2,1)} %param.8), channel_id=1, source_target_pairs={{16,0},{32,16},{48,32},{64,48},{80,64},{96,80},{112,96},{128,112},... | collective-permute-start | bytes 1376264 | tf_op jit(solution)/shard_map/ppermute | solution.py:31
  33.4 11.4 %collective-permute-start.2 = (bf16[128,1792]{1,0:T(8,128)(2,1)}, bf16[128,1792]{1,0:T(8,128)(2,1)S(1)}, u32[]{:S(2)}, u32[]{:S(2)}) collective-permute-start(bf16[128,1792]{1,0:T(8,128)(2,1)} %collective-permute-done.1), channel_id=1, source_target_pairs={{0,16},{16,32},{32,48},{48,64},{64,80},{80,96},{96,112},{112,128},... | collective-permute-start | bytes 1376264 | tf_op jit(solution)/shard_map/ppermute | solution.py:26
  33.4 0.8 copy-start.1
  34.2 10.7 %collective-permute-start.9 = (bf16[128,1792]{1,0:T(8,128)(2,1)S(1)}, bf16[128,1792]{1,0:T(8,128)(2,1)S(1)}, u32[]{:S(2)}, u32[]{:S(2)}) collective-permute-start(bf16[128,1792]{1,0:T(8,128)(2,1)S(1)} %collective-permute-done.8), channel_id=1, source_target_pairs={{16,0},{32,16},{48,32},{64,48},{80,64},{96,80},{112,96},{128,112},... | collective-permute-start | bytes 1376264 | tf_op jit(solution)/shard_map/ppermute | solution.py:31
  44.8 11.0 %copy-start.4 = (bf16[128,1792]{1,0:T(8,128)(2,1)}, bf16[128,1792]{1,0:T(8,128)(2,1)S(1)}, u32[]{:S(2)}) copy-start(bf16[128,1792]{1,0:T(8,128)(2,1)S(1)} %collective-permute-done.2) | copy-start | bytes 1376260
  44.8 10.6 %collective-permute-start.3 = (bf16[128,1792]{1,0:T(8,128)(2,1)S(1)}, bf16[128,1792]{1,0:T(8,128)(2,1)S(1)}, u32[]{:S(2)}, u32[]{:S(2)}) collective-permute-start(bf16[128,1792]{1,0:T(8,128)(2,1)S(1)} %collective-permute-done.2), channel_id=1, source_target_pairs={{0,16},{16,32},{32,48},{48,64},{64,80},{80,96},{96,112},{112,128},... | collective-permute-start | bytes 1376264 | tf_op jit(solution)/shard_map/ppermute | solution.py:26
  44.8 0.8 copy-start.2
  45.6 10.2 %collective-permute-start.10 = (bf16[128,1792]{1,0:T(8,128)(2,1)S(1)}, bf16[128,1792]{1,0:T(8,128)(2,1)S(1)}, u32[]{:S(2)}, u32[]{:S(2)}) collective-permute-start(bf16[128,1792]{1,0:T(8,128)(2,1)S(1)} %collective-permute-done.9), channel_id=1, source_target_pairs={{16,0},{32,16},{48,32},{64,48},{80,64},{96,80},{112,96},{128,112},... | collective-permute-start | bytes 1376264 | tf_op jit(solution)/shard_map/ppermute | solution.py:31
  55.4 23.4 %copy-start.9 = (bf16[128,1792]{1,0:T(8,128)(2,1)}, bf16[128,1792]{1,0:T(8,128)(2,1)S(1)}, u32[]{:S(2)}) copy-start(bf16[128,1792]{1,0:T(8,128)(2,1)S(1)} %collective-permute-done.3) | copy-start | bytes 1376260
  55.5 10.6 %collective-permute-start.4 = (bf16[128,1792]{1,0:T(8,128)(2,1)S(1)}, bf16[128,1792]{1,0:T(8,128)(2,1)S(1)}, u32[]{:S(2)}, u32[]{:S(2)}) collective-permute-start(bf16[128,1792]{1,0:T(8,128)(2,1)S(1)} %collective-permute-done.3), channel_id=1, source_target_pairs={{0,16},{16,32},{32,48},{48,64},{64,80},{80,96},{96,112},{112,128},... | collective-permute-start | bytes 1376264 | tf_op jit(solution)/shard_map/ppermute | solution.py:26
  55.8 5.2 %copy-start.5 = (bf16[128,1792]{1,0:T(8,128)(2,1)}, bf16[128,1792]{1,0:T(8,128)(2,1)S(1)}, u32[]{:S(2)}) copy-start(bf16[128,1792]{1,0:T(8,128)(2,1)S(1)} %collective-permute-done.10) | copy-start | bytes 1376260
  55.8 11.0 %collective-permute-start.11 = (bf16[128,1792]{1,0:T(8,128)(2,1)S(1)}, bf16[128,1792]{1,0:T(8,128)(2,1)S(1)}, u32[]{:S(2)}, u32[]{:S(2)}) collective-permute-start(bf16[128,1792]{1,0:T(8,128)(2,1)S(1)} %collective-permute-done.10), channel_id=1, source_target_pairs={{16,0},{32,16},{48,32},{64,48},{80,64},{96,80},{112,96},{128,112},... | collective-permute-start | bytes 1376264 | tf_op jit(solution)/shard_map/ppermute | solution.py:31
  66.1 18.1 %copy-start.10 = (bf16[128,1792]{1,0:T(8,128)(2,1)}, bf16[128,1792]{1,0:T(8,128)(2,1)S(1)}, u32[]{:S(2)}) copy-start(bf16[128,1792]{1,0:T(8,128)(2,1)S(1)} %collective-permute-done.4) | copy-start | bytes 1376260
  66.1 11.6 %collective-permute-start.5 = (bf16[128,1792]{1,0:T(8,128)(2,1)S(1)}, bf16[128,1792]{1,0:T(8,128)(2,1)S(1)}, u32[]{:S(2)}, u32[]{:S(2)}) collective-permute-start(bf16[128,1792]{1,0:T(8,128)(2,1)S(1)} %collective-permute-done.4), channel_id=1, source_target_pairs={{0,16},{16,32},{32,48},{48,64},{64,80},{80,96},{96,112},{112,128},... | collective-permute-start | bytes 1376264 | tf_op jit(solution)/shard_map/ppermute | solution.py:26
  67.5 11.3 %collective-permute-start.12 = (bf16[128,1792]{1,0:T(8,128)(2,1)S(1)}, bf16[128,1792]{1,0:T(8,128)(2,1)}, u32[]{:S(2)}, u32[]{:S(2)}) collective-permute-start(bf16[128,1792]{1,0:T(8,128)(2,1)S(1)} %collective-permute-done.11), channel_id=1, source_target_pairs={{16,0},{32,16},{48,32},{64,48},{80,64},{96,80},{112,96},{128,112},... | collective-permute-start | bytes 1376264 | tf_op jit(solution)/shard_map/ppermute | solution.py:31
  77.7 12.7 %copy-start.11 = (bf16[128,1792]{1,0:T(8,128)(2,1)}, bf16[128,1792]{1,0:T(8,128)(2,1)S(1)}, u32[]{:S(2)}) copy-start(bf16[128,1792]{1,0:T(8,128)(2,1)S(1)} %collective-permute-done.5) | copy-start | bytes 1376260
  77.7 12.7 %collective-permute-start.6 = (bf16[128,1792]{1,0:T(8,128)(2,1)S(1)}, bf16[128,1792]{1,0:T(8,128)(2,1)}, u32[]{:S(2)}, u32[]{:S(2)}) collective-permute-start(bf16[128,1792]{1,0:T(8,128)(2,1)S(1)} %collective-permute-done.5), channel_id=1, source_target_pairs={{0,16},{16,32},{32,48},{48,64},{64,80},{80,96},{96,112},{112,128},... | collective-permute-start | bytes 1376264 | tf_op jit(solution)/shard_map/ppermute | solution.py:26
  78.8 13.2 %collective-permute-start.13 = (bf16[128,1792]{1,0:T(8,128)(2,1)}, bf16[128,1792]{1,0:T(8,128)(2,1)}, u32[]{:S(2)}, u32[]{:S(2)}) collective-permute-start(bf16[128,1792]{1,0:T(8,128)(2,1)} %collective-permute-done.12), channel_id=1, source_target_pairs={{16,0},{32,16},{48,32},{64,48},{80,64},{96,80},{112,96},{128,112},... | collective-permute-start | bytes 1376264 | tf_op jit(solution)/shard_map/ppermute | solution.py:31
  90.4 13.7 %collective-permute-start.7 = (bf16[128,1792]{1,0:T(8,128)(2,1)}, bf16[128,1792]{1,0:T(8,128)(2,1)}, u32[]{:S(2)}, u32[]{:S(2)}) collective-permute-start(bf16[128,1792]{1,0:T(8,128)(2,1)} %collective-permute-done.6), channel_id=1, source_target_pairs={{0,16},{16,32},{32,48},{48,64},{64,80},{80,96},{96,112},{112,128},... | collective-permute-start | bytes 1376264 | tf_op jit(solution)/shard_map/ppermute | solution.py:26
  92.1 41.6 %collective-permute-start.14 = (bf16[128,1792]{1,0:T(8,128)(2,1)}, bf16[128,1792]{1,0:T(8,128)(2,1)}, u32[]{:S(2)}, u32[]{:S(2)}) collective-permute-start(bf16[128,1792]{1,0:T(8,128)(2,1)} %collective-permute-done.13), channel_id=1, source_target_pairs={{16,0},{32,16},{48,32},{64,48},{80,64},{96,80},{112,96},{128,112},... | collective-permute-start | bytes 1376264 | tf_op jit(solution)/shard_map/ppermute | solution.py:31
  112.7 158.7 %reduce-scatter.7.cloned.1.call-start = ((), (), s32[]{:S(2)}) async-start(), calls=%async_computation.6 | async-start | bytes 7798784 | tf_op jit(solution)/shard_map/reduce_scatter | solution.py:41
  112.8 14.8 %copy-start.3 = (bf16[128,1792]{1,0:T(8,128)(2,1)S(1)}, bf16[128,1792]{1,0:T(8,128)(2,1)}, u32[]{:S(2)}) copy-start(bf16[128,1792]{1,0:T(8,128)(2,1)} %copy-done.2) | copy-start | bytes 1376260
  112.8 15.6 %copy-start.6 = (bf16[128,1792]{1,0:T(8,128)(2,1)S(1)}, bf16[128,1792]{1,0:T(8,128)(2,1)}, u32[]{:S(2)}) copy-start(bf16[128,1792]{1,0:T(8,128)(2,1)} %copy-done.5) | copy-start | bytes 1376260
  112.8 16.4 %copy-start.8 = (bf16[128,1792]{1,0:T(8,128)(2,1)S(1)}, bf16[128,1792]{1,0:T(8,128)(2,1)}, u32[]{:S(2)}) copy-start(bf16[128,1792]{1,0:T(8,128)(2,1)} %copy-done.7) | copy-start | bytes 1376260
  163.2 109.9 %copy-start.12 = (s32[16]{0:T(128)S(1)}, s32[16]{0:T(128)}, u32[]{:S(2)}) copy-start(s32[16]{0:T(128)} %param.13) | copy-start | bytes 196
  163.3 161.3 %all-gather.8.cloned.1.call-start = ((), (), s32[]{:S(2)}) async-start(), calls=%async_computation.5 | async-start | bytes 2228224 | tf_op jit(solution)/shard_map/all_gather | solution.py:58
  203.5 165.2 %all-gather.4.cloned.1.call-start = ((), (), s32[]{:S(2)}) async-start(), calls=%async_computation.2 | async-start | bytes 3899392 | tf_op jit(solution)/shard_map/all_gather | solution.py:49
  (1 other events, 0.8 us)
Sparse Core Ops, SparseCore 0:
  21.0 45.1 all-gather.5
  112.8 89.0 reduce-scatter.4
  204.6 66.7 reduce-scatter.6
  274.0 50.5 all-gather.7
  326.4 42.2 all-gather.3
